TPU v7x, 512 devices: a whole 4x4x16 slice. The times are simulated.
512 devices in a mesh: dp: 32 (over y, x, core), tensor: 16 (over z).
Axes of the slice: x: 4, y: 4, z: 16, core: 2. Of those that a mesh axis runs over, the one named last changes fastest.
Arguments:
- rows_in: bfloat16 [16384, 8192], P('dp', 'tensor'), may hold values from -6 to 6
- adapter_ids: int32 [16384], P('dp'), may hold values from 0 to 511, as said below
- row_counts: int32 [32], P('dp'), may hold values from 256 to 512, as said below
- adapter_slot: int32 [512], replicated, may hold values from 0 to 511, each once
- adapter_a: bfloat16 [512, 16, 16], P(('dp', 'tensor')), may hold values from -1.5 to 1.5
- adapter_b: bfloat16 [512, 512, 1792], P(('dp', 'tensor')), may hold values from -0.25 to 0.25
Outputs:
- delta: bfloat16 [16384, 28672], P('dp', 'tensor')
Inputs may be any that keep to these rules, and one draw needn't show every extreme that they name: `adapter_ids`: within the 512 rows of one dp group (live or not), every adapter that is named is named by exactly 2 rows; some adapter is named by 2 live rows in every group. The live rows of a group are its first row_counts rows; some group has all 512 rows live. `adapter_slot`: each storage index appears once; storage index s is held by the device whose flattened dp, tensor index is s.
All inputs are finite; a program needn't handle non-finite values.
Results may differ from a plain program's by a relative error of at most 0.0049.
Values may be sent and summed in bfloat16 or wider, within the bound.
A program may use at most 128 MiB of HBM per device.

v0:
```python
import jax
import jax.numpy as jnp
from jax import lax
from jax.sharding import PartitionSpec as P

FA = 16
BIN = 512
BOUT = 1792


def on_device(rows_in, adapter_ids, row_counts, adapter_slot, adapter_a, adapter_b):
    group_count = lax.axis_size("dp")
    tensor_count = lax.axis_size("tensor")
    owner_count = group_count * tensor_count
    group_rows, feature_cols = rows_in.shape
    cap = max(2, group_rows // owner_count)
    catalog = jnp.arange(adapter_slot.shape[0], dtype=jnp.int32)
    id_match = adapter_ids[:, None] == catalog[None, :]
    owner_dev = jnp.sum(jnp.where(id_match, adapter_slot[None, :], 0), axis=1)
    position = jnp.arange(group_rows, dtype=jnp.int32)
    row_live = position < row_counts[0]
    earlier_same = (
        (owner_dev[:, None] == owner_dev[None, :])
        & (position[None, :] < position[:, None])
        & row_live[None, :]
    )
    slot_rank = jnp.sum(earlier_same.astype(jnp.int32), axis=1)
    slot_index = owner_dev * cap + slot_rank
    target = jnp.where(row_live, slot_index, owner_count * cap)
    buffer = (
        jnp.zeros((owner_count * cap, feature_cols), jnp.bfloat16)
        .at[target]
        .set(rows_in, mode="drop")
    )
    buffer = buffer.reshape(group_count, tensor_count, cap, feature_cols)
    arrived = lax.all_to_all(
        lax.all_to_all(buffer, "dp", split_axis=0, concat_axis=0, tiled=True),
        "tensor",
        split_axis=1,
        concat_axis=3,
        tiled=True,
    )
    whole_rows = arrived.reshape(group_count * cap, FA, BIN)
    mixed = jnp.einsum(
        "rij,ik->rkj", whole_rows, adapter_a[0], preferred_element_type=jnp.float32
    ).astype(jnp.bfloat16)
    result = jnp.dot(
        mixed.reshape(group_count * cap * FA, BIN), adapter_b[0], preferred_element_type=jnp.float32
    )
    result = result.astype(jnp.bfloat16).reshape(group_count, 1, cap, FA * BOUT)
    split_back = lax.all_to_all(result, "tensor", split_axis=3, concat_axis=1, tiled=True)
    returned = lax.all_to_all(split_back, "dp", split_axis=0, concat_axis=0, tiled=True)
    returned = returned.reshape(owner_count * cap, returned.shape[3])
    picked = jnp.take(returned, jnp.where(row_live, slot_index, 0), axis=0)
    return jnp.where(row_live[:, None], picked, jnp.zeros_like(picked))


def solution(mesh):
    return jax.shard_map(
        on_device,
        mesh=mesh,
        in_specs=(
            P("dp", "tensor"),
            P("dp"),
            P("dp"),
            P(),
            P(("dp", "tensor"), None, None),
            P(("dp", "tensor"), None, None),
        ),
        out_specs=P("dp", "tensor"),
        check_vma=False,
    )
```

profile of v0, /device:TPU:1, one launch (start us, length us, event | category | flops | bytes accessed | tf_op | source)
XLA Modules:
  0.0 457.6 jit_solution(2098749917473446583)
XLA Ops:
  0.0 0.0 copy-start
  0.8 0.9 select_reduce_fusion
  1.7 0.3 convert_reduce_fusion
  2.1 3.2 scatter_custom_fusion
  5.3 1.2 reshape.90
  6.5 27.7 %all_to_all.43 = bf16[32,16,2,512]{3,2,1,0:T(2,128)(2,1)S(1)} all-to-all(bf16[32,16,2,512]{3,2,1,0:T(2,128)(2,1)} %reshape.90), channel_id=1, replica_groups=mesh['dp'=32,'tensor'=16] {'dp'}, dimensions={0} | all-to-all | bytes 2097152 | tf_op jit(solution)/shard_map/all_to_all | solution.py:37
  34.2 1.0 copy.22
  35.2 0.0 copy-start.2
  35.2 58.0 %all_to_all.44 = bf16[32,16,2,512]{3,2,0,1:T(2,128)(2,1)S(1)} all-to-all(bf16[32,16,2,512]{3,2,0,1:T(2,128)(2,1)S(1)} %copy.22), channel_id=1, replica_groups=mesh['dp'=32,'tensor'=16] {'tensor'}, dimensions={1} | all-to-all | bytes 2097152 | tf_op jit(solution)/shard_map/all_to_all | solution.py:36
  93.2 0.9 copy.23
  94.0 0.0 copy-done.2
  94.1 0.5 convolution_convert_fusion.1
  94.5 0.0 copy-done
  94.6 3.9 convolution_convert_fusion
  98.4 8.4 %reshape.93 = bf16[32,1,2,28672]{3,2,0,1:T(2,128)(2,1)} reshape(bf16[1024,1792]{1,0:T(8,128)(2,1)} %convolution_convert_fusion) | data formatting | bytes 7340032 | tf_op jit(solution)/shard_map/reshape | solution.py:50
  106.8 34.8 %copy.25 = bf16[32,1,2,28672]{0,2,1,3:T(2,128)(2,1)} copy(bf16[32,1,2,28672]{3,2,0,1:T(2,128)(2,1)} %reshape.93) | data formatting | bytes 7340032 | tf_op jit(solution)/shard_map/reshape | solution.py:50
  141.7 19.3 %reshape.114 = bf16[16,2,57344]{2,1,0:T(2,128)(2,1)} reshape(bf16[28672,1,2,32]{3,2,1,0:T(2,128)(2,1)} %bitcast.30) | data formatting | bytes 7340032
  161.0 170.6 %all_to_all.45 = bf16[16,2,57344]{2,1,0:T(2,128)(2,1)} all-to-all(bf16[16,2,57344]{2,1,0:T(2,128)(2,1)} %reshape.114), channel_id=1, replica_groups=mesh['dp'=32,'tensor'=16] {'tensor'}, dimensions={0} | all-to-all | bytes 7340032 | tf_op jit(solution)/shard_map/all_to_all | solution.py:51
  331.5 15.6 %reshape.115 = bf16[28672,1,2,32]{3,2,1,0:T(2,128)(2,1)} reshape(bf16[16,2,57344]{2,1,0:T(2,128)(2,1)} %all_to_all.45) | data formatting | bytes 7340032
  347.1 35.1 %copy.26 = bf16[32,1,2,16,1792]{4,2,3,0,1:T(2,128)(2,1)} copy(bf16[32,1,2,16,1792]{0,2,4,3,1:T(2,128)(2,1)} %bitcast.31) | data formatting | bytes 7340032 | tf_op jit(solution)/shard_map/all_to_all | solution.py:51
  382.2 11.7 %all-to-all-start.3 = ((bf16[32,16,2,1792]{3,2,1,0:T(2,128)(2,1)}), bf16[32,16,2,1792]{3,2,1,0:T(2,128)(2,1)}, u32[]{:S(2)}, u32[]{:S(2)}) async-start(bf16[32,16,2,1792]{3,2,1,0:T(2,128)(2,1)} %bitcast.32), calls=%async_computation.3 | async-start | bytes 7340032 | tf_op jit(solution)/shard_map/all_to_all | solution.py:52
  393.9 44.7 %all-to-all-done.3 = bf16[32,16,2,1792]{3,2,1,0:T(2,128)(2,1)} async-done(((bf16[32,16,2,1792]{3,2,1,0:T(2,128)(2,1)}), bf16[32,16,2,1792]{3,2,1,0:T(2,128)(2,1)}, u32[]{:S(2)}, u32[]{:S(2)}) %all-to-all-start.3) | async-done | bytes 3670048 | tf_op jit(solution)/shard_map/all_to_all | solution.py:52
  438.6 8.6 %reshape.94 = bf16[1024,1792]{1,0:T(8,128)(2,1)} reshape(bf16[32,16,2,1792]{3,2,1,0:T(2,128)(2,1)} %all-to-all-done.3) | data formatting | bytes 7340032 | tf_op jit(solution)/shard_map/reshape | solution.py:53
  447.2 7.3 %gather_fusion = bf16[512,1792]{1,0:T(8,128)(2,1)} fusion(bf16[1024,1792]{1,0:T(8,128)(2,1)} %reshape.94, s32[1024]{0:T(1024)S(1)} %pad_clamp_fusion), kind=kCustom, calls=%fused_computation | custom fusion | bytes 3672064 | tf_op jit(solution)/shard_map/jit(_take)/gather | solution.py:54
  454.5 0.0 copy-start.1
  454.5 3.2 select_select_fusion
  457.6 0.0 copy-done.1
  (4 shorter events, 0.0 us)
Async XLA Ops:
  0.0 94.5 %copy-start = (bf16[1,512,1792]{2,1,0:T(8,128)(2,1)S(1)}, bf16[1,512,1792]{2,1,0:T(8,128)(2,1)}, u32[]{:S(2)}) copy-start(bf16[1,512,1792]{2,1,0:T(8,128)(2,1)} %param.11) | copy-start | bytes 5505028
  35.2 58.8 %copy-start.2 = (bf16[1,16,16]{2,1,0:T(8,128)(2,1)S(1)}, bf16[1,16,16]{2,1,0:T(8,128)(2,1)}, u32[]{:S(2)}) copy-start(bf16[1,16,16]{2,1,0:T(8,128)(2,1)} %param.10) | copy-start | bytes 1540
  382.2 56.4 %all-to-all-start.3 = ((bf16[32,16,2,1792]{3,2,1,0:T(2,128)(2,1)}), bf16[32,16,2,1792]{3,2,1,0:T(2,128)(2,1)}, u32[]{:S(2)}, u32[]{:S(2)}) async-start(bf16[32,16,2,1792]{3,2,1,0:T(2,128)(2,1)} %bitcast.32), calls=%async_computation.3 | async-start | bytes 7340032 | tf_op jit(solution)/shard_map/all_to_all | solution.py:52
  454.5 3.2 copy-start.1
where the time goes:
time: 464 us; the launch traced here: 458 us
  blocking collectives  256 us (55%)
  local copies, waits for them, and re-layouts  135 us (29%)
  waiting for transfers between devices  44.7 us (10%)
  starting transfers between devices  11.7 us (3%)
    all_to_all x1, blocking collectives, on_device(): lax.all_to_all(result, 'tensor', split_axis=3, concat_axis=1, tiled=True)  171 us
    all_to_all x1, blocking collectives, on_device(): lax.all_to_all(lax.all_to_all(buffer, 'dp', split_axis=0, concat_axis=0,...  58 us
    all_to_all x1, waiting for transfers between devices, on_device(): lax.all_to_all(split_back, 'dp', split_axis=0, concat_axis=0, tiled=True)  44.7 us
    reshape x2, local copies, waits for them, and re-layouts, on_device(): result = result.astype(jnp.bfloat16).reshape(group_count, 1, cap, FA * BOUT)  43.3 us
    all_to_all x1, local copies, waits for them, and re-layouts, on_device(): lax.all_to_all(result, 'tensor', split_axis=3, concat_axis=1, tiled=True)  35.1 us
    unnamed x8, local copies, waits for them, and re-layouts  34.9 us
    all_to_all x1, blocking collectives, on_device(): lax.all_to_all(buffer, 'dp', split_axis=0, concat_axis=0, tiled=True)  27.7 us
    all_to_all x1, starting transfers between devices, on_device(): lax.all_to_all(split_back, 'dp', split_axis=0, concat_axis=0, tiled=True)  11.7 us
  transfers between devices with their start and end apart: 1, of which 1 were waited for; matrix products, arithmetic and copies ran while one was open for 0% of the time, Pallas kernels for 0%

commit v1 on v0

v1 whole, which is shorter than its diff:
```python
import functools

import jax
import jax.numpy as jnp
from jax import lax
from jax.experimental import pallas as pl
from jax.experimental.pallas import tpu as pltpu
from jax.sharding import PartitionSpec as P

CAP = 2
IN_CHUNK = 128
OUT_CHUNK = 256
ROW_BLOCK = 256
MESH = pl.DeviceIdType.MESH


def one_hot(mask):
    return jnp.where(mask, 1.0, 0.0).astype(jnp.bfloat16)


def dot(left, right):
    return jnp.dot(left, right, preferred_element_type=jnp.float32)


def exchange_kernel(
    n_dp,
    n_t,
    width,
    row_block,
    cs_row_ref,
    kc_row_ref,
    kc_col_ref,
    cs_col_ref,
    x_ref,
    mix_ref,
    b_ref,
    out_ref,
    pack_mat,
    spread_mat,
    gather_mat,
    place_mat,
    in_z_src,
    in_z_dst,
    in_d_src,
    in_d_dst,
    mixed,
    out_d_src,
    out_d_dst,
    out_z_src,
    out_z_dst,
    in_z_send,
    in_z_recv,
    in_d_send,
    in_d_recv,
    out_d_send,
    out_d_recv,
    out_z_send,
    out_z_recv,
):
    g = lax.axis_index("dp")
    t = lax.axis_index("tensor")
    in_chunks, packed, in_cols = in_z_src.shape
    out_chunks, slots, out_cols = out_d_src.shape
    per_group = slots // n_dp
    rows = x_ref.shape[0]

    barrier = pltpu.get_barrier_semaphore()

    def greet_t(step, carry):
        pl.semaphore_signal(
            barrier, inc=1, device_id=(g, lax.rem(t + step, n_t)), device_id_type=MESH
        )
        return carry

    def greet_d(step, carry):
        pl.semaphore_signal(
            barrier, inc=1, device_id=(lax.rem(g + step, n_dp), t), device_id_type=MESH
        )
        return carry

    lax.fori_loop(1, n_t, greet_t, 0)
    lax.fori_loop(1, n_dp, greet_d, 0)

    def blocks(total, body):
        size = min(row_block, total)

        def step(at, carry):
            body(pl.multiple_of(at * size, size), size)
            return carry

        lax.fori_loop(0, total // size, step, 0)

    def z_distance(step):
        half = (step + 1) // 2
        return n_t // 2 + jnp.where(step % 2 == 1, half, -half)

    def send_z(src, dst, chunk, send_sem, recv_sem):
        def step(at, carry):
            peer = lax.rem(t + z_distance(at), n_t)
            pltpu.make_async_remote_copy(
                src_ref=src.at[chunk, pl.ds(pl.multiple_of(peer * width, width), width)],
                dst_ref=dst.at[chunk, pl.ds(pl.multiple_of(t * width, width), width)],
                send_sem=send_sem.at[chunk],
                recv_sem=recv_sem.at[chunk],
                device_id=(g, peer),
                device_id_type=MESH,
            ).start()
            return carry

        lax.fori_loop(0, n_t - 1, step, 0)
        own = pl.ds(pl.multiple_of(t * width, width), width)
        pltpu.make_async_copy(
            src.at[chunk, own], dst.at[chunk, own], recv_sem.at[chunk]
        ).start()

    def send_d(src, dst, chunk, send_sem, recv_sem):
        def step(at, carry):
            peer = lax.rem(g + at, n_dp)
            pltpu.make_async_remote_copy(
                src_ref=src.at[chunk, pl.ds(pl.multiple_of(peer * per_group, per_group), per_group)],
                dst_ref=dst.at[chunk, pl.ds(pl.multiple_of(g * per_group, per_group), per_group)],
                send_sem=send_sem.at[chunk],
                recv_sem=recv_sem.at[chunk],
                device_id=(peer, t),
                device_id_type=MESH,
            ).start()
            return carry

        lax.fori_loop(1, n_dp, step, 0)
        own = pl.ds(pl.multiple_of(g * per_group, per_group), per_group)
        pltpu.make_async_copy(
            src.at[chunk, own], dst.at[chunk, own], recv_sem.at[chunk]
        ).start()

    def arrived(dst, chunk, recv_sem):
        pltpu.make_async_copy(dst.at[chunk], dst.at[chunk], recv_sem.at[chunk]).wait()

    def sent(src, count, chunks, send_sem):
        def step(chunk, carry):
            part = src.at[chunk, pl.ds(0, count)]
            pltpu.make_async_copy(part, part, send_sem.at[chunk]).wait()
            return carry

        lax.fori_loop(0, chunks, step, 0)

    def fill_pack(at, size):
        index = lax.broadcasted_iota(jnp.int32, (size, rows), 0) + at
        pack_mat[pl.ds(at, size), :] = one_hot(index == cs_row_ref[...])

    blocks(packed, fill_pack)

    def pack_chunk(chunk):
        columns = pl.ds(pl.multiple_of(chunk * in_cols, in_cols), in_cols)

        def body(at, size):
            in_z_src[chunk, pl.ds(at, size), :] = dot(
                pack_mat[pl.ds(at, size), :], x_ref[:, columns]
            ).astype(jnp.bfloat16)

        blocks(packed, body)

    pack_chunk(0)
    pl.semaphore_wait(barrier, n_dp + n_t - 2)

    def start_in(chunk, carry):
        send_z(in_z_src, in_z_dst, chunk, in_z_send, in_z_recv)

        @pl.when(chunk < in_chunks - 1)
        def _():
            pack_chunk(chunk + 1)

        return carry

    lax.fori_loop(0, in_chunks, start_in, 0)

    def fill_spread(at, size):
        index = lax.broadcasted_iota(jnp.int32, (size, packed), 0) + at
        spread_mat[pl.ds(at, size), :] = one_hot(index == kc_row_ref[...])

    def fill_gather(at, size):
        index = lax.broadcasted_iota(jnp.int32, (size, slots), 1)
        gather_mat[pl.ds(at, size), :] = one_hot(index == kc_col_ref[pl.ds(at, size), :])

    def fill_place(at, size):
        index = lax.broadcasted_iota(jnp.int32, (size, packed), 1)
        place_mat[pl.ds(at, size), :] = one_hot(index == cs_col_ref[pl.ds(at, size), :])

    blocks(slots, fill_spread)
    blocks(packed, fill_gather)
    blocks(rows, fill_place)

    def spread_chunk(chunk, carry):
        arrived(in_z_dst, chunk, in_z_recv)

        def body(at, size):
            in_d_src[chunk, pl.ds(at, size), :] = dot(
                spread_mat[pl.ds(at, size), :], in_z_dst[chunk]
            ).astype(jnp.bfloat16)

        blocks(slots, body)
        send_d(in_d_src, in_d_dst, chunk, in_d_send, in_d_recv)
        return carry

    lax.fori_loop(0, in_chunks, spread_chunk, 0)

    for chunk in range(in_chunks):
        arrived(in_d_dst, chunk, in_d_recv)

        def mix(at, size):
            mixed[pl.ds(at, size), chunk * in_cols : (chunk + 1) * in_cols] = dot(
                mix_ref[...], in_d_dst[chunk, pl.ds(at, size), :]
            ).astype(jnp.bfloat16)

        blocks(slots, mix)

    def start_out(chunk):
        columns = pl.ds(pl.multiple_of(chunk * out_cols, out_cols), out_cols)

        def body(at, size):
            out_d_src[chunk, pl.ds(at, size), :] = dot(
                mixed[pl.ds(at, size), :], b_ref[:, columns]
            ).astype(jnp.bfloat16)

        blocks(slots, body)
        send_d(out_d_src, out_d_dst, chunk, out_d_send, out_d_recv)

    start_out(0)
    start_out(1)

    def relay(chunk, carry):
        arrived(out_d_dst, chunk, out_d_recv)

        def body(at, size):
            out_z_src[chunk, pl.ds(at, size), :] = dot(
                gather_mat[pl.ds(at, size), :], out_d_dst[chunk]
            ).astype(jnp.bfloat16)

        blocks(packed, body)
        send_z(out_z_src, out_z_dst, chunk, out_z_send, out_z_recv)

        @pl.when(chunk + 2 < out_chunks)
        def _():
            start_out(chunk + 2)

        return carry

    lax.fori_loop(0, out_chunks, relay, 0)

    def place(chunk, carry):
        arrived(out_z_dst, chunk, out_z_recv)
        columns = pl.ds(pl.multiple_of(chunk * out_cols, out_cols), out_cols)

        def body(at, size):
            out_ref[pl.ds(at, size), columns] = dot(
                place_mat[pl.ds(at, size), :], out_z_dst[chunk]
            ).astype(jnp.bfloat16)

        blocks(rows, body)
        return carry

    lax.fori_loop(0, out_chunks, place, 0)

    sent(in_z_src, (n_t - 1) * width, in_chunks, in_z_send)
    sent(in_d_src, (n_dp - 1) * per_group, in_chunks, in_d_send)
    sent(out_d_src, (n_dp - 1) * per_group, out_chunks, out_d_send)
    sent(out_z_src, (n_t - 1) * width, out_chunks, out_z_send)


def on_device(rows_in, adapter_ids, row_counts, adapter_slot, adapter_a, adapter_b):
    n_dp = lax.axis_size("dp")
    n_t = lax.axis_size("tensor")
    rows, in_width = rows_in.shape
    order = adapter_a.shape[1]
    out_width = adapter_b.shape[2]
    width = n_dp * CAP
    packed = n_t * width
    per_group = order * CAP
    slots = n_dp * per_group
    row_block = min(ROW_BLOCK, slots)

    catalog = jnp.arange(adapter_slot.shape[0], dtype=jnp.int32)
    owner = jnp.sum(
        jnp.where(adapter_ids[:, None] == catalog[None, :], adapter_slot[None, :], 0), axis=1
    )
    position = jnp.arange(rows, dtype=jnp.int32)
    live = position < row_counts[0]
    earlier = position[None, :] < position[:, None]
    rank = jnp.sum(
        ((adapter_ids[:, None] == adapter_ids[None, :]) & earlier).astype(jnp.int32), axis=1
    )
    column = owner % n_t
    place = jnp.sum(
        ((column[:, None] == column[None, :]) & earlier & live[None, :]).astype(jnp.int32), axis=1
    )
    packed_at = jnp.where(live, column * width + place, -1)
    slot_at = (owner // n_t) * per_group + rank
    mine = lax.axis_index("tensor") * width + jnp.arange(width, dtype=jnp.int32)
    key = (
        jnp.sum(jnp.where(packed_at[:, None] == mine[None, :], slot_at[:, None] + 1, 0), axis=0) - 1
    )
    step = jnp.arange(order, dtype=jnp.int32) * CAP
    keys = jnp.where(key[None, :] >= 0, key[None, :] + step[:, None], -1).reshape(packed)

    at = jnp.arange(row_block, dtype=jnp.int32)
    unit = (at // CAP) % order
    pick = (unit[:, None] == jnp.arange(order, dtype=jnp.int32)[None, :]).astype(jnp.bfloat16)
    wide = jnp.dot(jnp.dot(pick, adapter_a[0].T), pick.T)
    same = (at[:, None] // per_group == at[None, :] // per_group) & (
        at[:, None] % CAP == at[None, :] % CAP
    )
    mix = jnp.where(same, wide, jnp.zeros_like(wide))

    in_chunks = max(1, in_width // IN_CHUNK)
    in_cols = in_width // in_chunks
    out_chunks = max(2, out_width // OUT_CHUNK)
    out_cols = out_width // out_chunks
    dma = pltpu.SemaphoreType.DMA
    bf16 = jnp.bfloat16
    return pl.pallas_call(
        functools.partial(exchange_kernel, n_dp, n_t, width, row_block),
        out_shape=jax.ShapeDtypeStruct((rows, out_width), bf16),
        in_specs=[pl.BlockSpec(memory_space=pltpu.VMEM)] * 7,
        out_specs=pl.BlockSpec(memory_space=pltpu.VMEM),
        scratch_shapes=[
            pltpu.VMEM((packed, rows), bf16),
            pltpu.VMEM((slots, packed), bf16),
            pltpu.VMEM((packed, slots), bf16),
            pltpu.VMEM((rows, packed), bf16),
            pltpu.VMEM((in_chunks, packed, in_cols), bf16),
            pltpu.VMEM((in_chunks, packed, in_cols), bf16),
            pltpu.VMEM((in_chunks, slots, in_cols), bf16),
            pltpu.VMEM((in_chunks, slots, in_cols), bf16),
            pltpu.VMEM((slots, in_width), bf16),
            pltpu.VMEM((out_chunks, slots, out_cols), bf16),
            pltpu.VMEM((out_chunks, slots, out_cols), bf16),
            pltpu.VMEM((out_chunks, packed, out_cols), bf16),
            pltpu.VMEM((out_chunks, packed, out_cols), bf16),
            dma((in_chunks,)),
            dma((in_chunks,)),
            dma((in_chunks,)),
            dma((in_chunks,)),
            dma((out_chunks,)),
            dma((out_chunks,)),
            dma((out_chunks,)),
            dma((out_chunks,)),
        ],
        compiler_params=pltpu.CompilerParams(
            collective_id=0, has_side_effects=True, vmem_limit_bytes=56 * 1024 * 1024
        ),
        cost_estimate=pl.CostEstimate(
            flops=2 * slots * in_width * out_width, bytes_accessed=10_000_000, transcendentals=0
        ),
    )(
        packed_at[None, :],
        keys[None, :],
        keys[:, None],
        packed_at[:, None],
        rows_in,
        mix,
        adapter_b[0],
    )


def solution(mesh):
    return jax.shard_map(
        on_device,
        mesh=mesh,
        in_specs=(
            P("dp", "tensor"),
            P("dp"),
            P("dp"),
            P(),
            P(("dp", "tensor"), None, None),
            P(("dp", "tensor"), None, None),
        ),
        out_specs=P("dp", "tensor"),
        check_vma=False,
    )
```

time: 464 us -> 259 us (0.56); the launches traced: 458 us -> 258 us
  blocking collectives: 256 us -> 0 us
  Pallas kernels: 0 us -> 248 us
  local copies, waits for them, and re-layouts: 135 us -> 5.08 us
  waiting for transfers between devices: 44.7 us -> 0 us
  starting transfers between devices: 11.7 us -> 0 us
    all_to_all x3 -> x0, blocking collectives: 256 us -> none  [the longest x1 171 us: on_device(): lax.all_to_all(result, 'tensor', split_axis=3, concat_axis=1, tiled=True)]
    pallas_call x0 -> x1, Pallas kernels: none -> 248 us  [on_device(): pl.pallas_call(functools.partial(exchange_kernel, n_dp, n_t, width, row_b...]
    reshape x4 -> x0, local copies, waits for them, and re-layouts: 53.1 us -> none  [the longest x2 43.3 us: on_device(): result = result.astype(jnp.bfloat16).reshape(group_count, 1, cap, FA * BOUT)]
    all_to_all x1 -> x0, waiting for transfers between devices: 44.7 us -> none  [on_device(): lax.all_to_all(split_back, 'dp', split_axis=0, concat_axis=0, tiled=True)]
    all_to_all x3 -> x0, local copies, waits for them, and re-layouts: 36.9 us -> none  [the longest x1 35.1 us: on_device(): lax.all_to_all(result, 'tensor', split_axis=3, concat_axis=1, tiled=True)]
    unnamed x8 -> x3, local copies, waits for them, and re-layouts: 34.9 us -> 2.85 us
    all_to_all x1 -> x0, starting transfers between devices: 11.7 us -> none  [on_device(): lax.all_to_all(split_back, 'dp', split_axis=0, concat_axis=0, tiled=True)]
    gather x1 -> x0, local copies, waits for them, and re-layouts: 7.26 us -> none  [on_device(): picked = jnp.take(returned, jnp.where(row_live, slot_index, 0), axis=0)]
  transfers between devices with their start and end apart: 1 -> 0, of which waited for: 1 -> 0; matrix products, arithmetic and copies ran while one was open for 0% -> 0% of each run, Pallas kernels for 0% -> 0%
where the time goes in v1:
time: 259 us; the launch traced here: 258 us
  Pallas kernels  248 us (96%)
  local copies, waits for them, and re-layouts  5.08 us (2%)
  other arithmetic  3.15 us (1%)
    pallas_call x1, Pallas kernels, on_device(): pl.pallas_call(functools.partial(exchange_kernel, n_dp, n_t, width, row_b...  248 us

profile of v1, /device:TPU:1, one launch (start us, length us, event | category | flops | bytes accessed | tf_op | source)
XLA Modules:
  0.0 258.4 jit_solution(4331163312396661413)
XLA Ops:
  0.0 0.0 copy-start
  0.7 1.1 convert_reduce_fusion
  1.9 0.3 convert_reduce_fusion.1
  2.1 0.6 compare_select_fusion.2.cs_row_ref
  2.7 0.2 select_reduce_fusion.1
  2.9 0.1 add_select_fusion.1
  3.0 0.7 select_n.169.kc_row_ref
  3.7 0.0 copy-done
  3.7 1.1 convolution_select_fusion.mix_ref
  4.8 0.1 copy.15
  5.0 0.1 copy.12
  5.1 0.9 fusion.8.cs_col_ref
  6.0 1.3 select_n.178.kc_col_ref
  7.2 248.3 %shard_map.64 = bf16[512,1792]{1,0:T(8,128)(2,1)} custom-call(s32[1,512]{1,0:T(1,128)} %compare_select_fusion.2.cs_row_ref, s32[1,1024]{1,0:T(1,128)} %select_n.169.kc_row_ref, s32[1024,1]{1,0:T(8,128)} %select_n.178.kc_col_ref, s32[512,1]{1,0:T(8,128)} %fusion.8.cs_col_ref, bf16[512,512]{1,0:T(8,128)(2,1)} %x_ref.1, ...), custom_call_target="tpu_custom_call" | custom-call | flops 1879048192 | bytes 10000000 | tf_op jit(solution)/shard_map/pallas_call | solution.py:319
  255.5 2.8 %copy.19 = bf16[512,1792]{1,0:T(8,128)(2,1)} copy(bf16[512,1792]{1,0:T(8,128)(2,1)} %shard_map.64) | data formatting | bytes 3670016
  (9 shorter events, 0.1 us)
Async XLA Ops:
  0.0 3.7 %copy-start = (bf16[1,16,16]{2,1,0:T(8,128)(2,1)S(1)}, bf16[1,16,16]{2,1,0:T(8,128)(2,1)}, u32[]{:S(2)}) copy-start(bf16[1,16,16]{2,1,0:T(8,128)(2,1)} %param.10) | copy-start | bytes 1540

commit v2 on v1

--- a/solution.py
+++ b/solution.py
@@ -22,19 +22,97 @@
     return jnp.dot(left, right, preferred_element_type=jnp.float32)
 
 
+def plan_kernel(
+    n_dp, n_t, per_group, ids_ref, slot_ref, count_ref, rows_ref, cols_ref, most_ref,
+    mine, peers, send_sem, recv_sem
+):
+    g = lax.axis_index("dp")
+    t = lax.axis_index("tensor")
+    rows = ids_ref.shape[1]
+    tile = mine.shape[0]
+    barrier = pltpu.get_barrier_semaphore()
+
+    def greet(step, carry):
+        pl.semaphore_signal(
+            barrier, inc=1, device_id=(lax.rem(g + step, n_dp), t), device_id_type=MESH
+        )
+        return carry
+
+    lax.fori_loop(1, n_dp, greet, 0)
+    down = lax.broadcasted_iota(jnp.int32, (rows, rows), 0)
+    across = lax.broadcasted_iota(jnp.int32, (rows, rows), 1)
+
+    def turned(row):
+        return jnp.sum(jnp.where(down == across, row, 0), axis=1, keepdims=True)
+
+    def counted(mask, axis):
+        return jnp.sum(jnp.where(mask, 1, 0), axis=axis, keepdims=True)
+
+    ids = ids_ref[...]
+    ids_col = turned(ids)
+    owner_col = jnp.sum(jnp.where(ids_col == across, slot_ref[...], 0), axis=1, keepdims=True)
+    owner = jnp.sum(jnp.where(down == across, owner_col, 0), axis=0, keepdims=True)
+    live = across < count_ref[...]
+    live_col = down < count_ref[...]
+    column = lax.rem(owner, n_t)
+    column_col = lax.rem(owner_col, n_t)
+    alike = column_col == column
+    place = counted(alike & (down < across) & live_col, 0)
+    lane = lax.broadcasted_iota(jnp.int32, (1, rows), 1)
+    is_live = lane < count_ref[...]
+    width = CAP * n_dp
+    code = jnp.where(is_live, column * width + place, -1)
+    most = jnp.max(jnp.where(is_live, place + 1, 0), axis=1, keepdims=True)
+    mine[...] = jnp.broadcast_to(most.astype(jnp.float32), mine.shape)
+
+    pl.semaphore_wait(barrier, n_dp - 1)
+
+    def send(step, carry):
+        peer = lax.rem(g + step, n_dp)
+        pltpu.make_async_remote_copy(
+            src_ref=mine,
+            dst_ref=peers.at[pl.ds(pl.multiple_of(g * tile, tile), tile)],
+            send_sem=send_sem,
+            recv_sem=recv_sem,
+            device_id=(peer, t),
+            device_id_type=MESH,
+        ).start()
+        return carry
+
+    lax.fori_loop(1, n_dp, send, 0)
+    pltpu.make_async_copy(
+        mine, peers.at[pl.ds(pl.multiple_of(g * tile, tile), tile)], recv_sem
+    ).start()
+
+    same = ids_col == ids
+    slot_at = lax.div(owner, n_t) * per_group + counted(same & (down < across), 0)
+    rows_ref[0:1, :] = code
+    rows_ref[1:2, :] = slot_at
+    place_col = counted(alike & (across < down) & live, 1)
+    index = lax.broadcasted_iota(jnp.int32, (rows, 1), 0)
+    code_col = jnp.where(index < count_ref[...], column_col * width + place_col, -1)
+    slot_col = lax.div(owner_col, n_t) * per_group + counted(same & (across < down), 1)
+    side = lax.broadcasted_iota(jnp.int32, cols_ref.shape, 1)
+    cols_ref[...] = jnp.where(side == 0, code_col, slot_col)
+
+    pltpu.make_async_copy(peers, peers, recv_sem).wait()
+    most_ref[...] = jnp.max(peers[...], axis=0, keepdims=True).astype(jnp.int32)
+    part = peers.at[pl.ds(0, (n_dp - 1) * tile)]
+    pltpu.make_async_copy(part, part, send_sem).wait()
+
+
 def exchange_kernel(
     n_dp,
     n_t,
     width,
     row_block,
-    cs_row_ref,
-    kc_row_ref,
-    kc_col_ref,
-    cs_col_ref,
+    rows_ref,
+    cols_ref,
     x_ref,
-    mix_ref,
+    a_ref,
     b_ref,
     out_ref,
+    mix_mat,
     pack_mat,
     spread_mat,
     gather_mat,
@@ -143,9 +221,19 @@
 
         lax.fori_loop(0, chunks, step, 0)
 
+    full = CAP * n_dp
+
+    def repack(code):
+        return jnp.where(code >= 0, lax.div(code, full) * width + lax.rem(code, full), -1)
+
+    code = rows_ref[0:1, :]
+    code_col = cols_ref[:, 0:1]
+    packed_at = repack(code)
+    packed_at_col = repack(code_col)
+
     def fill_pack(at, size):
         index = lax.broadcasted_iota(jnp.int32, (size, rows), 0) + at
-        pack_mat[pl.ds(at, size), :] = one_hot(index == cs_row_ref[...])
+        pack_mat[pl.ds(at, size), :] = one_hot(index == packed_at)
 
     blocks(packed, fill_pack)
 
@@ -173,17 +261,50 @@
 
     lax.fori_loop(0, in_chunks, start_in, 0)
 
+    order = a_ref.shape[0]
+    first = t * width
+    spot = lax.broadcasted_iota(jnp.int32, (1, packed), 1)
+    key = jnp.sum(
+        jnp.where(packed_at_col == first + lax.rem(spot, width), cols_ref[:, 1:2] + 1, 0),
+        axis=0,
+        keepdims=True,
+    )
+    key = jnp.where(key > 0, key - 1 + lax.div(spot, width) * CAP, -1)
+
     def fill_spread(at, size):
         index = lax.broadcasted_iota(jnp.int32, (size, packed), 0) + at
-        spread_mat[pl.ds(at, size), :] = one_hot(index == kc_row_ref[...])
+        spread_mat[pl.ds(at, size), :] = one_hot(index == key)
 
     def fill_gather(at, size):
+        spot = lax.broadcasted_iota(jnp.int32, (size, 1), 0) + at
+        key = jnp.sum(
+            jnp.where(packed_at == first + lax.rem(spot, width), rows_ref[1:2, :] + 1, 0),
+            axis=1,
+            keepdims=True,
+        )
+        key = jnp.where(key > 0, key - 1 + lax.div(spot, width) * CAP, -1)
         index = lax.broadcasted_iota(jnp.int32, (size, slots), 1)
-        gather_mat[pl.ds(at, size), :] = one_hot(index == kc_col_ref[pl.ds(at, size), :])
+        gather_mat[pl.ds(at, size), :] = one_hot(index == key)
 
     def fill_place(at, size):
         index = lax.broadcasted_iota(jnp.int32, (size, packed), 1)
-        place_mat[pl.ds(at, size), :] = one_hot(index == cs_col_ref[pl.ds(at, size), :])
+        target = repack(cols_ref[pl.ds(at, size), 0:1])
+        place_mat[pl.ds(at, size), :] = one_hot(index == target)
+
+    side = mix_mat.shape[0]
+    unit = lax.rem(lax.div(lax.broadcasted_iota(jnp.int32, (side, order), 0), CAP), order)
+    pick = one_hot(unit == lax.broadcasted_iota(jnp.int32, (side, order), 1))
+    contract = (((1,), (1,)), ((), ()))
+    tall = lax.dot_general(pick, a_ref[...], contract, preferred_element_type=jnp.float32)
+    wide = lax.dot_general(
+        tall.astype(jnp.bfloat16), pick, contract, preferred_element_type=jnp.float32
+    )
+    down = lax.broadcasted_iota(jnp.int32, (side, side), 0)
+    across = lax.broadcasted_iota(jnp.int32, (side, side), 1)
+    same = (lax.div(down, per_group) == lax.div(across, per_group)) & (
+        lax.rem(down, CAP) == lax.rem(across, CAP)
+    )
+    mix_mat[...] = jnp.where(same, wide, 0.0).astype(jnp.bfloat16)
 
     blocks(slots, fill_spread)
     blocks(packed, fill_gather)
@@ -208,7 +329,7 @@
 
         def mix(at, size):
             mixed[pl.ds(at, size), chunk * in_cols : (chunk + 1) * in_cols] = dot(
-                mix_ref[...], in_d_dst[chunk, pl.ds(at, size), :]
+                mix_mat[...], in_d_dst[chunk, pl.ds(at, size), :]
             ).astype(jnp.bfloat16)
 
         blocks(slots, mix)
@@ -266,50 +387,15 @@
     sent(out_z_src, (n_t - 1) * width, out_chunks, out_z_send)
 
 
-def on_device(rows_in, adapter_ids, row_counts, adapter_slot, adapter_a, adapter_b):
+def exchange(width, collective_id, row_plan, col_plan, rows_in, small, large):
     n_dp = lax.axis_size("dp")
     n_t = lax.axis_size("tensor")
     rows, in_width = rows_in.shape
-    order = adapter_a.shape[1]
-    out_width = adapter_b.shape[2]
-    width = n_dp * CAP
+    order = small.shape[0]
+    out_width = large.shape[1]
     packed = n_t * width
-    per_group = order * CAP
-    slots = n_dp * per_group
+    slots = n_dp * order * CAP
     row_block = min(ROW_BLOCK, slots)
-
-    catalog = jnp.arange(adapter_slot.shape[0], dtype=jnp.int32)
-    owner = jnp.sum(
-        jnp.where(adapter_ids[:, None] == catalog[None, :], adapter_slot[None, :], 0), axis=1
-    )
-    position = jnp.arange(rows, dtype=jnp.int32)
-    live = position < row_counts[0]
-    earlier = position[None, :] < position[:, None]
-    rank = jnp.sum(
-        ((adapter_ids[:, None] == adapter_ids[None, :]) & earlier).astype(jnp.int32), axis=1
-    )
-    column = owner % n_t
-    place = jnp.sum(
-        ((column[:, None] == column[None, :]) & earlier & live[None, :]).astype(jnp.int32), axis=1
-    )
-    packed_at = jnp.where(live, column * width + place, -1)
-    slot_at = (owner // n_t) * per_group + rank
-    mine = lax.axis_index("tensor") * width + jnp.arange(width, dtype=jnp.int32)
-    key = (
-        jnp.sum(jnp.where(packed_at[:, None] == mine[None, :], slot_at[:, None] + 1, 0), axis=0) - 1
-    )
-    step = jnp.arange(order, dtype=jnp.int32) * CAP
-    keys = jnp.where(key[None, :] >= 0, key[None, :] + step[:, None], -1).reshape(packed)
-
-    at = jnp.arange(row_block, dtype=jnp.int32)
-    unit = (at // CAP) % order
-    pick = (unit[:, None] == jnp.arange(order, dtype=jnp.int32)[None, :]).astype(jnp.bfloat16)
-    wide = jnp.dot(jnp.dot(pick, adapter_a[0].T), pick.T)
-    same = (at[:, None] // per_group == at[None, :] // per_group) & (
-        at[:, None] % CAP == at[None, :] % CAP
-    )
-    mix = jnp.where(same, wide, jnp.zeros_like(wide))
-
     in_chunks = max(1, in_width // IN_CHUNK)
     in_cols = in_width // in_chunks
     out_chunks = max(2, out_width // OUT_CHUNK)
@@ -319,9 +405,10 @@
     return pl.pallas_call(
         functools.partial(exchange_kernel, n_dp, n_t, width, row_block),
         out_shape=jax.ShapeDtypeStruct((rows, out_width), bf16),
-        in_specs=[pl.BlockSpec(memory_space=pltpu.VMEM)] * 7,
+        in_specs=[pl.BlockSpec(memory_space=pltpu.VMEM)] * 5,
         out_specs=pl.BlockSpec(memory_space=pltpu.VMEM),
         scratch_shapes=[
+            pltpu.VMEM((row_block, row_block), bf16),
             pltpu.VMEM((packed, rows), bf16),
             pltpu.VMEM((slots, packed), bf16),
             pltpu.VMEM((packed, slots), bf16),
@@ -345,18 +432,51 @@
             dma((out_chunks,)),
         ],
         compiler_params=pltpu.CompilerParams(
-            collective_id=0, has_side_effects=True, vmem_limit_bytes=56 * 1024 * 1024
+            collective_id=collective_id,
+            has_side_effects=True,
+            vmem_limit_bytes=56 * 1024 * 1024,
         ),
         cost_estimate=pl.CostEstimate(
             flops=2 * slots * in_width * out_width, bytes_accessed=10_000_000, transcendentals=0
         ),
-    )(
-        packed_at[None, :],
-        keys[None, :],
-        keys[:, None],
-        packed_at[:, None],
+    )(row_plan, col_plan, rows_in, small, large)
+
+
+def on_device(rows_in, adapter_ids, row_counts, adapter_slot, adapter_a, adapter_b):
+    n_dp = lax.axis_size("dp")
+    n_t = lax.axis_size("tensor")
+    rows = rows_in.shape[0]
+    order = adapter_a.shape[1]
+    i32 = jnp.int32
+    row_plan, col_plan, most = pl.pallas_call(
+        functools.partial(plan_kernel, n_dp, n_t, order * CAP),
+        out_shape=(
+            jax.ShapeDtypeStruct((2, rows), i32),
+            jax.ShapeDtypeStruct((rows, 2), i32),
+            jax.ShapeDtypeStruct((1, 128), i32),
+        ),
+        in_specs=[pl.BlockSpec(memory_space=pltpu.VMEM)] * 3,
+        out_specs=[pl.BlockSpec(memory_space=pltpu.VMEM)] * 3,
+        scratch_shapes=[
+            pltpu.VMEM((8, 128), jnp.float32),
+            pltpu.VMEM((8 * n_dp, 128), jnp.float32),
+            pltpu.SemaphoreType.DMA,
+            pltpu.SemaphoreType.DMA,
+        ],
+        compiler_params=pltpu.CompilerParams(
+            collective_id=0, has_side_effects=True, vmem_limit_bytes=32 * 1024 * 1024
+        ),
+    )(adapter_ids[None, :], adapter_slot[None, :], row_counts[None, :])
+    full = CAP * n_dp
+    tight = full * 3 // 4
+    return lax.cond(
+        most[0, 0] <= tight,
+        functools.partial(exchange, tight, 1),
+        functools.partial(exchange, full, 2),
+        row_plan,
+        col_plan,
         rows_in,
-        mix,
+        adapter_a[0],
         adapter_b[0],
     )
 

time: 259 us -> 208 us (0.80)
  Pallas kernels: 248 us -> 205 us
  other arithmetic: 3.15 us -> 0 us
    pallas_call x1 -> x2, Pallas kernels: 248 us -> 205 us  [the longest x1 189 us: exchange(): pl.pallas_call(functools.partial(exchange_kernel, n_dp, n_t, width, row_b...]
where the time goes in v2:
time: 208 us
  Pallas kernels  205 us (99%)
  local copies, waits for them, and re-layouts  2.59 us (1%)
    pallas_call x1, Pallas kernels, exchange(): pl.pallas_call(functools.partial(exchange_kernel, n_dp, n_t, width, row_b...  189 us
    pallas_call x1, Pallas kernels, on_device(): pl.pallas_call(functools.partial(plan_kernel, n_dp, n_t, order * CAP), ou...  15.5 us

profile of v2, /device:TPU:1, one launch (start us, length us, event | category | flops | bytes accessed | tf_op | source)
XLA Modules:
  0.0 208.0 jit_solution(14333871358207018953)
XLA Ops:
  0.7 0.0 copy-start
  0.7 0.7 copy-done
  1.3 0.0 copy-start.1
  1.3 0.7 copy-done.1
  2.0 15.5 %shard_map.66 = (s32[2,512]{1,0:T(2,128)S(1)}, s32[512,2]{1,0:T(8,128)S(1)}, s32[1,128]{1,0:T(1,128)S(1)}) custom-call(s32[1,512]{1,0:T(1,128)S(1)} %bitcast.8, s32[1,512]{1,0:T(1,128)S(1)} %bitcast.9, s32[1,1]{1,0:T(1,128)} %bitcast.7.count_ref), custom_call_target="tpu_custom_call" | custom-call | tf_op jit(solution)/shard_map/pallas_call | solution.py:451
  17.5 189.2 %conditional.1 = (bf16[512,1792]{1,0:T(8,128)(2,1)S(1)}) conditional(s32[]{:T(128)} %bitcast.3, (s32[2,512]{1,0:T(2,128)S(1)}, s32[512,2]{1,0:T(8,128)S(1)}, bf16[512,512]{1,0:T(8,128)(2,1)}, bf16[16,16]{1,0:T(8,128)(2,1)}, bf16[512,1792]{1,0:T(8,128)(2,1)}) %tuple.18, (s32[2,512]{1,0:T(2,128)S(1)}, s32[512,2]{1,0:T(8,128)S(1)}, ...), branch_computations={%region_0.0_spmd, %region_1.0_spmd} | conditional | flops 1879048192 | bytes 10000008 | solution.py:472
  17.5 189.2 %branch_1_fun.1 = bf16[512,1792]{1,0:T(8,128)(2,1)S(1)} custom-call(s32[2,512]{1,0:T(2,128)S(1)} %get-tuple-element.33.rows_ref, s32[512,2]{1,0:T(8,128)S(1)} %get-tuple-element.34.cols_ref, bf16[512,512]{1,0:T(8,128)(2,1)} %get-tuple-element.35.x_ref, bf16[16,16]{1,0:T(8,128)(2,1)} %get-tuple-element.36.a_ref, bf16[512,1792]{1,0:T(8,128)(2,1)} %get-tuple-element.37.b_ref), custom_call_target="tpu_custom_call" | custom-call | flops 1879048192 | bytes 10000000 | tf_op jit(solution)/shard_map/cond/branch_1_fun/pallas_call | solution.py:405
  206.8 1.2 copy.13
Async XLA Ops:
  0.7 0.7 copy-start
  1.3 0.7 copy-start.1

commit v3 on v0

v3 whole, which is shorter than its diff:
```python
import functools

import jax
import jax.numpy as jnp
from jax import lax
from jax.experimental import pallas as pl
from jax.experimental.pallas import tpu as pltpu
from jax.sharding import PartitionSpec as P

RANKS = 2
IN_CHUNK = 128
OUT_CHUNK = 256
SIDE = 256
MESH = pl.DeviceIdType.MESH
BF16 = jnp.bfloat16
I32 = jnp.int32


def one_hot(mask):
    return jnp.where(mask, 1.0, 0.0).astype(BF16)


def dot(left, right):
    return jnp.dot(left, right, preferred_element_type=jnp.float32)


def iota(shape, axis):
    return lax.broadcasted_iota(I32, shape, axis)


def total(parts):
    return functools.reduce(lambda a, b: a + b, parts)


class Plan:
    def __init__(self, n_dp, rest):
        full = n_dp * RANKS
        self.tight = full * 3 // 4
        self.rest = rest
        if rest:
            self.width = full - self.tight
            self.ranks = (1,)
            self.in_stages = ((0, self.width),)
            self.out_stages = ((0, self.width),)
            self.sources = {1: (0,)}
            self.needs = ((1,),)
        else:
            self.width = self.tight
            self.ranks = (0, 1)
            self.in_stages = ((0, n_dp), (n_dp, self.width))
            self.out_stages = ((0, self.width - n_dp), (self.width - n_dp, self.width))
            self.sources = {0: (0,), 1: (0, 1)}
            self.needs = ((0,), (0, 1))


def exchange_kernel(n_dp, n_t, plan, ids_ref, slot_ref, count_ref, x_ref, a_ref, b_ref, *refs):
    if plan.rest:
        out_ref, mix_mat, ins, mids, outs = refs
        flag = None
    else:
        out_ref, over_ref, mix_mat, ins, mids, outs, flag = refs
    g = lax.axis_index("dp")
    t = lax.axis_index("tensor")
    rows = x_ref.shape[0]
    order = a_ref.shape[0]
    lines = n_dp * order
    width = plan.width
    in_chunks, _, in_cols = ins[0]["src"].shape
    out_chunks, _, out_cols = outs[0]["src"].shape

    barrier = pltpu.get_barrier_semaphore()

    def greet_t(step, carry):
        pl.semaphore_signal(
            barrier, inc=1, device_id=(g, lax.rem(t + step, n_t)), device_id_type=MESH
        )
        return carry

    def greet_d(step, carry):
        pl.semaphore_signal(
            barrier, inc=1, device_id=(lax.rem(g + step, n_dp), t), device_id_type=MESH
        )
        return carry

    lax.fori_loop(1, n_t, greet_t, 0)
    lax.fori_loop(1, n_dp, greet_d, 0)

    def send_z(part, chunk, height):
        src, dst, send_sem, recv_sem = part["src"], part["dst"], part["send"], part["recv"]

        def step(at, carry):
            half = (at + 1) // 2
            distance = n_t // 2 + jnp.where(at % 2 == 1, half, -half)
            peer = lax.rem(t + distance, n_t)
            pltpu.make_async_remote_copy(
                src_ref=src.at[chunk, pl.ds(pl.multiple_of(peer * height, height), height)],
                dst_ref=dst.at[chunk, pl.ds(pl.multiple_of(t * height, height), height)],
                send_sem=send_sem.at[chunk],
                recv_sem=recv_sem.at[chunk],
                device_id=(g, peer),
                device_id_type=MESH,
            ).start()
            return carry

        lax.fori_loop(0, n_t - 1, step, 0)
        own = pl.ds(pl.multiple_of(t * height, height), height)
        pltpu.make_async_copy(
            src.at[chunk, own], dst.at[chunk, own], recv_sem.at[chunk]
        ).start()

    def send_d(src, dst, chunk, send_sem, recv_sem):
        def step(at, carry):
            peer = lax.rem(g + at, n_dp)
            pltpu.make_async_remote_copy(
                src_ref=src.at[chunk, pl.ds(pl.multiple_of(peer * order, order), order)],
                dst_ref=dst.at[chunk, pl.ds(pl.multiple_of(g * order, order), order)],
                send_sem=send_sem.at[chunk],
                recv_sem=recv_sem.at[chunk],
                device_id=(peer, t),
                device_id_type=MESH,
            ).start()
            return carry

        lax.fori_loop(1, n_dp, step, 0)
        own = pl.ds(pl.multiple_of(g * order, order), order)
        pltpu.make_async_copy(
            src.at[chunk, own], dst.at[chunk, own], recv_sem.at[chunk]
        ).start()

    def arrived(dst, chunk, recv_sem):
        pltpu.make_async_copy(dst.at[chunk], dst.at[chunk], recv_sem.at[chunk]).wait()

    def sent(src, height, send_sem):
        chunks, tall, _ = src.shape

        def step(chunk, carry):
            part = src.at[chunk, pl.ds(0, tall - height)]
            pltpu.make_async_copy(part, part, send_sem.at[chunk]).wait()
            return carry

        lax.fori_loop(0, chunks, step, 0)

    def in_columns(chunk):
        return pl.ds(pl.multiple_of(chunk * in_cols, in_cols), in_cols)

    def out_columns(chunk):
        return pl.ds(pl.multiple_of(chunk * out_cols, out_cols), out_cols)

    down = iota((rows, rows), 0)
    across = iota((rows, rows), 1)
    diagonal = down == across
    before = down < across

    def to_column(row):
        return jnp.sum(jnp.where(diagonal, row, 0), axis=1, keepdims=True)

    def to_row(column):
        return jnp.sum(jnp.where(diagonal, column, 0), axis=0, keepdims=True)

    def count(mask):
        return jnp.sum(jnp.where(mask, 1, 0), axis=0, keepdims=True)

    ids = ids_ref[...]
    ids_col = to_column(ids)
    owner_col = jnp.sum(jnp.where(ids_col == across, slot_ref[...], 0), axis=1, keepdims=True)
    rank = count((ids_col == ids) & before)
    owner = to_row(owner_col)
    column = lax.rem(owner, n_t)
    team = column * RANKS + rank
    team_col = to_column(team)
    live = iota((1, rows), 1) < count_ref[...]
    earlier = count((team_col == team) & before)
    firsts = count((team_col == column * RANKS) & (down < count_ref[...]))
    top = plan.tight - 1 - earlier
    over = live & (rank == 1) & (top < firsts)
    if plan.rest:
        code = jnp.where(over, column * width + firsts - 1 - top, -1)
    else:
        place = jnp.where(rank == 1, top, earlier)
        code = jnp.where(live & ~over, column * width + place, -1)

    def pack(stage, chunk):
        ins[stage]["src"][chunk] = dot(ins[stage]["pack"][...], x_ref[:, in_columns(chunk)]).astype(
            BF16
        )

    for stage, (lo, hi) in enumerate(plan.in_stages):
        height = hi - lo
        spot = iota((n_t * height, 1), 0)
        spot = lax.div(spot, height) * width + lo + lax.rem(spot, height)
        ins[stage]["pack"][...] = one_hot(spot == code)
        if stage == 0:
            pack(0, 0)
            pl.semaphore_wait(barrier, n_dp + n_t - 2)

        def start_in(chunk, carry, stage=stage, height=height):
            if stage > 0:
                pack(stage, chunk)
            send_z(ins[stage], chunk, height)
            if stage == 0:

                @pl.when(chunk < in_chunks - 1)
                def _():
                    pack(0, chunk + 1)

            return carry

        lax.fori_loop(0, in_chunks, start_in, 0)

    if flag is not None:
        tile = flag["src"].shape[0]
        most = jnp.max(jnp.where(over, 1.0, 0.0), axis=1, keepdims=True)
        flag["src"][...] = jnp.broadcast_to(most, flag["src"].shape)
        spot = pl.ds(pl.multiple_of(g * tile, tile), tile)

        def tell(step, carry):
            pltpu.make_async_remote_copy(
                src_ref=flag["src"],
                dst_ref=flag["dst"].at[spot],
                send_sem=flag["send"],
                recv_sem=flag["recv"],
                device_id=(lax.rem(g + step, n_dp), t),
                device_id_type=MESH,
            ).start()
            return carry

        lax.fori_loop(1, n_dp, tell, 0)
        pltpu.make_async_copy(flag["src"], flag["dst"].at[spot], flag["recv"]).start()

    code_col = to_column(code)
    rank_col = lax.rem(team_col, RANKS)
    line = lax.div(owner, n_t) * order + 1
    line_col = lax.div(owner_col, n_t) * order + 1
    first = t * width

    def build_spread(half):
        mid = mids[plan.ranks.index(half)]
        for at, stage in enumerate(plan.sources[half]):
            lo, hi = plan.in_stages[stage]
            height = hi - lo
            lane = iota((1, n_t * height), 1)
            here = (code_col == first + lo + lax.rem(lane, height)) & (rank_col == half)
            key = jnp.sum(jnp.where(here, line_col, 0), axis=0, keepdims=True)
            key = jnp.where(key > 0, key - 1 + lax.div(lane, height), -1)
            mid["spread"][at][...] = one_hot(iota((lines, n_t * height), 0) == key)

    def build_gather(stage):
        lo, hi = plan.out_stages[stage]
        height = hi - lo
        spot = iota((n_t * height, 1), 0)
        for at, half in enumerate(plan.needs[stage]):
            here = (code == first + lo + lax.rem(spot, height)) & (rank == half)
            key = jnp.sum(jnp.where(here, line, 0), axis=1, keepdims=True)
            key = jnp.where(key > 0, key - 1 + lax.div(spot, height), -1)
            outs[stage]["gather"][at][...] = one_hot(iota((n_t * height, lines), 1) == key)

    def build_place():
        for stage, (lo, hi) in enumerate(plan.out_stages):
            height = hi - lo
            lane = iota((1, n_t * height), 1)
            lane = lax.div(lane, height) * width + lo + lax.rem(lane, height)
            outs[stage]["place"][...] = one_hot(code_col == lane)

    def build_mix():
        side = mix_mat.shape[0]
        pick = one_hot(lax.rem(iota((side, order), 0), order) == iota((side, order), 1))
        contract = (((1,), (1,)), ((), ()))
        tall = lax.dot_general(pick, a_ref[...], contract, preferred_element_type=jnp.float32)
        wide = lax.dot_general(
            tall.astype(BF16), pick, contract, preferred_element_type=jnp.float32
        )
        same = lax.div(iota((side, side), 0), order) == lax.div(iota((side, side), 1), order)
        mix_mat[...] = jnp.where(same, wide, 0.0).astype(BF16)

    def spread(half):
        mid = mids[plan.ranks.index(half)]

        def step(chunk, carry):
            for stage in plan.sources[half]:
                if half == plan.ranks[0] or stage not in plan.sources[plan.ranks[0]]:
                    arrived(ins[stage]["dst"], chunk, ins[stage]["recv"])
            mid["in_src"][chunk] = total(
                dot(mid["spread"][at][...], ins[stage]["dst"][chunk])
                for at, stage in enumerate(plan.sources[half])
            ).astype(BF16)
            send_d(mid["in_src"], mid["in_dst"], chunk, mid["in_send"], mid["in_recv"])
            return carry

        lax.fori_loop(0, in_chunks, step, 0)

    def mix(half):
        mid = mids[plan.ranks.index(half)]
        side = mix_mat.shape[0]

        def step(chunk, carry):
            arrived(mid["in_dst"], chunk, mid["in_recv"])
            for at in range(0, lines, side):
                mid["mixed"][at : at + side, in_columns(chunk)] = dot(
                    mix_mat[...], mid["in_dst"][chunk, at : at + side, :]
                ).astype(BF16)
            return carry

        lax.fori_loop(0, in_chunks, step, 0)

    def start_out(half, chunk):
        mid = mids[plan.ranks.index(half)]
        mid["out_src"][chunk] = dot(mid["mixed"][...], b_ref[:, out_columns(chunk)]).astype(BF16)
        send_d(mid["out_src"], mid["out_dst"], chunk, mid["out_send"], mid["out_recv"])

    def relay(stage, start, stop):
        lo, hi = plan.out_stages[stage]
        half = plan.needs[stage][-1]
        mid = mids[plan.ranks.index(half)]

        def step(chunk, carry):
            arrived(mid["out_dst"], chunk, mid["out_recv"])
            outs[stage]["src"][chunk] = total(
                dot(
                    outs[stage]["gather"][at][...],
                    mids[plan.ranks.index(need)]["out_dst"][chunk],
                )
                for at, need in enumerate(plan.needs[stage])
            ).astype(BF16)
            send_z(outs[stage], chunk, hi - lo)

            @pl.when(chunk + 2 < out_chunks)
            def _():
                start_out(half, chunk + 2)

            return carry

        lax.fori_loop(start, stop, step, 0)

    head = plan.ranks[0]
    build_spread(head)
    build_mix()
    build_gather(0)
    spread(head)
    mix(head)
    start_out(head, 0)
    start_out(head, 1)
    if plan.rest:
        build_place()
        relay(0, 0, out_chunks)
    else:
        build_spread(1)
        relay(0, 0, 1)
        spread(1)
        relay(0, 1, 3)
        mix(1)
        build_gather(1)
        relay(0, 3, out_chunks - 1)
        start_out(1, 0)
        relay(0, out_chunks - 1, out_chunks)
        start_out(1, 1)
        build_place()
        relay(1, 0, out_chunks)

    def place_chunk(chunk, carry):
        for part in outs:
            arrived(part["dst"], chunk, part["recv"])
        out_ref[:, out_columns(chunk)] = total(
            dot(part["place"][...], part["dst"][chunk]) for part in outs
        ).astype(BF16)
        return carry

    lax.fori_loop(0, out_chunks, place_chunk, 0)

    if flag is not None:
        pltpu.make_async_copy(flag["dst"], flag["dst"], flag["recv"]).wait()
        over_ref[...] = jnp.max(flag["dst"][...], axis=0, keepdims=True).astype(I32)
        part = flag["dst"].at[pl.ds(0, (n_dp - 1) * flag["src"].shape[0])]
        pltpu.make_async_copy(part, part, flag["send"]).wait()
    for stage, (lo, hi) in enumerate(plan.in_stages):
        sent(ins[stage]["src"], hi - lo, ins[stage]["send"])
    for mid in mids:
        sent(mid["in_src"], order, mid["in_send"])
        sent(mid["out_src"], order, mid["out_send"])
    for stage, (lo, hi) in enumerate(plan.out_stages):
        sent(outs[stage]["src"], hi - lo, outs[stage]["send"])


def exchange(rest, ids, slot, counts, rows_in, small, large):
    n_dp = lax.axis_size("dp")
    n_t = lax.axis_size("tensor")
    plan = Plan(n_dp, rest)
    rows, in_width = rows_in.shape
    order = small.shape[0]
    out_width = large.shape[1]
    lines = n_dp * order
    side = min(SIDE, lines)
    in_chunks = max(1, in_width // IN_CHUNK)
    in_cols = in_width // in_chunks
    out_chunks = max(4, out_width // OUT_CHUNK)
    out_cols = out_width // out_chunks

    def sems(n):
        return pltpu.SemaphoreType.DMA((n,))

    def buffer(*shape):
        return pltpu.VMEM(shape, BF16)

    def in_scratch(lo, hi):
        tall = n_t * (hi - lo)
        return {
            "pack": buffer(tall, rows),
            "src": buffer(in_chunks, tall, in_cols),
            "dst": buffer(in_chunks, tall, in_cols),
            "send": sems(in_chunks),
            "recv": sems(in_chunks),
        }

    def mid_scratch(half):
        heights = [plan.in_stages[s][1] - plan.in_stages[s][0] for s in plan.sources[half]]
        return {
            "spread": [buffer(lines, n_t * height) for height in heights],
            "in_src": buffer(in_chunks, lines, in_cols),
            "in_dst": buffer(in_chunks, lines, in_cols),
            "mixed": buffer(lines, in_width),
            "out_src": buffer(out_chunks, lines, out_cols),
            "out_dst": buffer(out_chunks, lines, out_cols),
            "in_send": sems(in_chunks),
            "in_recv": sems(in_chunks),
            "out_send": sems(out_chunks),
            "out_recv": sems(out_chunks),
        }

    def out_scratch(stage):
        lo, hi = plan.out_stages[stage]
        tall = n_t * (hi - lo)
        return {
            "gather": [buffer(tall, lines) for _ in plan.needs[stage]],
            "place": buffer(rows, tall),
            "src": buffer(out_chunks, tall, out_cols),
            "dst": buffer(out_chunks, tall, out_cols),
            "send": sems(out_chunks),
            "recv": sems(out_chunks),
        }

    scratch = [
        buffer(side, side),
        [in_scratch(lo, hi) for lo, hi in plan.in_stages],
        [mid_scratch(half) for half in plan.ranks],
        [out_scratch(stage) for stage in range(len(plan.out_stages))],
    ]
    out_shape = [jax.ShapeDtypeStruct((rows, out_width), BF16)]
    if not rest:
        out_shape.append(jax.ShapeDtypeStruct((1, 128), I32))
        scratch.append(
            {
                "src": pltpu.VMEM((8, 128), jnp.float32),
                "dst": pltpu.VMEM((8 * n_dp, 128), jnp.float32),
                "send": pltpu.SemaphoreType.DMA,
                "recv": pltpu.SemaphoreType.DMA,
            }
        )
    return pl.pallas_call(
        functools.partial(exchange_kernel, n_dp, n_t, plan),
        out_shape=out_shape,
        in_specs=[pl.BlockSpec(memory_space=pltpu.VMEM)] * 6,
        out_specs=[pl.BlockSpec(memory_space=pltpu.VMEM)] * len(out_shape),
        scratch_shapes=scratch,
        compiler_params=pltpu.CompilerParams(
            collective_id=1 if rest else 0,
            has_side_effects=True,
            vmem_limit_bytes=56 * 1024 * 1024,
        ),
        cost_estimate=pl.CostEstimate(
            flops=2 * RANKS * lines * in_width * out_width,
            bytes_accessed=10_000_000,
            transcendentals=0,
        ),
    )(ids, slot, counts, rows_in, small, large)


def on_device(rows_in, adapter_ids, row_counts, adapter_slot, adapter_a, adapter_b):
    args = (
        adapter_ids[None, :],
        adapter_slot[None, :],
        row_counts[None, :],
        rows_in,
        adapter_a[0],
        adapter_b[0],
    )
    done, over = exchange(False, *args)
    return lax.cond(
        over[0, 0] > 0,
        lambda done, *args: done + exchange(True, *args)[0],
        lambda done, *args: done,
        done,
        *args,
    )


def solution(mesh):
    return jax.shard_map(
        on_device,
        mesh=mesh,
        in_specs=(
            P("dp", "tensor"),
            P("dp"),
            P("dp"),
            P(),
            P(("dp", "tensor"), None, None),
            P(("dp", "tensor"), None, None),
        ),
        out_specs=P("dp", "tensor"),
        check_vma=False,
    )
```

time: 464 us -> 185 us (0.40); the launches traced: 458 us -> 185 us
  blocking collectives: 256 us -> 0 us
  Pallas kernels: 0 us -> 182 us
  local copies, waits for them, and re-layouts: 135 us -> 1.25 us
  waiting for transfers between devices: 44.7 us -> 0 us
  starting transfers between devices: 11.7 us -> 0 us
    all_to_all x3 -> x0, blocking collectives: 256 us -> none  [the longest x1 171 us: on_device(): lax.all_to_all(result, 'tensor', split_axis=3, concat_axis=1, tiled=True)]
    pallas_call x0 -> x1, Pallas kernels: none -> 182 us  [exchange(): pl.pallas_call(functools.partial(exchange_kernel, n_dp, n_t, plan), out_s...]
    reshape x4 -> x0, local copies, waits for them, and re-layouts: 53.1 us -> none  [the longest x2 43.3 us: on_device(): result = result.astype(jnp.bfloat16).reshape(group_count, 1, cap, FA * BOUT)]
    all_to_all x1 -> x0, waiting for transfers between devices: 44.7 us -> none  [on_device(): lax.all_to_all(split_back, 'dp', split_axis=0, concat_axis=0, tiled=True)]
    all_to_all x3 -> x0, local copies, waits for them, and re-layouts: 36.9 us -> none  [the longest x1 35.1 us: on_device(): lax.all_to_all(result, 'tensor', split_axis=3, concat_axis=1, tiled=True)]
    unnamed x8 -> x11, local copies, waits for them, and re-layouts: 34.9 us -> 1.25 us
    all_to_all x1 -> x0, starting transfers between devices: 11.7 us -> none  [on_device(): lax.all_to_all(split_back, 'dp', split_axis=0, concat_axis=0, tiled=True)]
    gather x1 -> x0, local copies, waits for them, and re-layouts: 7.26 us -> none  [on_device(): picked = jnp.take(returned, jnp.where(row_live, slot_index, 0), axis=0)]
  transfers between devices with their start and end apart: 1 -> 0, of which waited for: 1 -> 0; matrix products, arithmetic and copies ran while one was open for 0% -> 0% of each run, Pallas kernels for 0% -> 0%
where the time goes in v3:
time: 185 us
  Pallas kernels  182 us (98%)
    pallas_call x1, Pallas kernels, exchange(): pl.pallas_call(functools.partial(exchange_kernel, n_dp, n_t, plan), out_s...  182 us

profile of v3, /device:TPU:1, one launch (start us, length us, event | category | flops | bytes accessed | tf_op | source)
XLA Modules:
  0.0 184.7 jit_solution(4096216962828102447)
XLA Ops:
  0.7 0.0 copy-start
  0.7 0.0 copy-start.1
  0.7 0.0 copy-start.2
  0.7 0.0 copy-start.3
  0.7 0.0 copy-start.4
  0.7 182.1 %shard_map.66 = (bf16[512,1792]{1,0:T(8,128)(2,1)S(1)}, s32[1,128]{1,0:T(1,128)}) custom-call(s32[1,512]{1,0:T(1,128)} %bitcast.12, s32[1,512]{1,0:T(1,128)} %bitcast.14, s32[1,1]{1,0:T(1,128)} %bitcast.7.count_ref, bf16[512,512]{1,0:T(8,128)(2,1)} %x_ref.1, bf16[16,16]{1,0:T(8,128)(2,1)} %bitcast.10, bf16[512,1792]{1,0:T(8,128)(2,1)} %bitcast.8), custom_call_target="tpu_custom_call" | custom-call | flops 1879048192 | bytes 10000000 | tf_op jit(solution)/shard_map/pallas_call | solution.py:457
  183.4 0.0 copy-done
  183.4 0.0 copy-done.1
  183.4 0.0 copy-done.2
  183.4 0.0 copy-done.3
  183.5 0.0 copy-done.4
  183.5 1.2 copy.13
  (1 shorter events, 0.0 us)
Async XLA Ops:
  0.7 182.8 %copy-start = (bf16[1,512,1792]{2,1,0:T(8,128)(2,1)S(1)}, bf16[1,512,1792]{2,1,0:T(8,128)(2,1)}, u32[]{:S(2)}) copy-start(bf16[1,512,1792]{2,1,0:T(8,128)(2,1)} %param.13) | copy-start | bytes 5505028
  0.7 182.8 %copy-start.1 = (bf16[512,512]{1,0:T(8,128)(2,1)S(1)}, bf16[512,512]{1,0:T(8,128)(2,1)}, u32[]{:S(2)}) copy-start(bf16[512,512]{1,0:T(8,128)(2,1)} %x_ref.1) | copy-start | bytes 1572868
  0.7 182.8 %copy-start.2 = (bf16[1,16,16]{2,1,0:T(8,128)(2,1)S(1)}, bf16[1,16,16]{2,1,0:T(8,128)(2,1)}, u32[]{:S(2)}) copy-start(bf16[1,16,16]{2,1,0:T(8,128)(2,1)} %param.12) | copy-start | bytes 1540
  0.7 182.8 %copy-start.3 = (s32[512]{0:T(512)S(1)}, s32[512]{0:T(512)}, u32[]{:S(2)}) copy-start(s32[512]{0:T(512)} %param.9) | copy-start | bytes 6148
  0.7 182.8 %copy-start.4 = (s32[512]{0:T(512)S(1)}, s32[512]{0:T(512)}, u32[]{:S(2)}) copy-start(s32[512]{0:T(512)} %param.11) | copy-start | bytes 6148

commit v4 on v3

v4 whole, which is shorter than its diff:
```python
import functools

import jax
import jax.numpy as jnp
from jax import lax
from jax.experimental import pallas as pl
from jax.experimental.pallas import tpu as pltpu
from jax.sharding import PartitionSpec as P

RANKS = 2
IN_CHUNK = 128
OUT_CHUNK = 256
SIDE = 256
MESH = pl.DeviceIdType.MESH
BF16 = jnp.bfloat16
I32 = jnp.int32


def one_hot(mask):
    return jnp.where(mask, 1.0, 0.0).astype(BF16)


def dot(left, right):
    return jnp.dot(left, right, preferred_element_type=jnp.float32)


def iota(shape, axis):
    return lax.broadcasted_iota(I32, shape, axis)


def total(parts):
    return functools.reduce(lambda a, b: a + b, parts)


class Plan:
    def __init__(self, n_dp, rest):
        full = n_dp * RANKS
        self.tight = full * 3 // 4
        self.rest = rest
        if rest:
            self.width = full - self.tight
            self.units = ((0, self.width, 1, IN_CHUNK),)
        else:
            self.width = self.tight
            split = self.width - n_dp
            self.units = ((0, split, 1, IN_CHUNK), (split, self.width, 2, 2 * IN_CHUNK))


def exchange_kernel(n_dp, n_t, plan, ids_ref, slot_ref, count_ref, x_ref, a_ref, b_ref, *refs):
    if plan.rest:
        out_ref, units = refs
        flag = None
    else:
        out_ref, over_ref, units, flag = refs
    g = lax.axis_index("dp")
    t = lax.axis_index("tensor")
    rows = x_ref.shape[0]
    order = a_ref.shape[0]
    width = plan.width
    out_chunks, _, out_cols = units[0]["back_z"]["src"].shape

    barrier = pltpu.get_barrier_semaphore()

    def greet_t(step, carry):
        pl.semaphore_signal(
            barrier, inc=1, device_id=(g, lax.rem(t + step, n_t)), device_id_type=MESH
        )
        return carry

    def greet_d(step, carry):
        pl.semaphore_signal(
            barrier, inc=1, device_id=(lax.rem(g + step, n_dp), t), device_id_type=MESH
        )
        return carry

    lax.fori_loop(1, n_t, greet_t, 0)
    lax.fori_loop(1, n_dp, greet_d, 0)

    def send_z(part, chunk, height):
        src, dst, send_sem, recv_sem = part["src"], part["dst"], part["send"], part["recv"]

        def step(at, carry):
            half = (at + 1) // 2
            distance = n_t // 2 + jnp.where(at % 2 == 1, half, -half)
            peer = lax.rem(t + distance, n_t)
            pltpu.make_async_remote_copy(
                src_ref=src.at[chunk, pl.ds(pl.multiple_of(peer * height, height), height)],
                dst_ref=dst.at[chunk, pl.ds(pl.multiple_of(t * height, height), height)],
                send_sem=send_sem.at[chunk],
                recv_sem=recv_sem.at[chunk],
                device_id=(g, peer),
                device_id_type=MESH,
            ).start()
            return carry

        lax.fori_loop(0, n_t - 1, step, 0)
        own = pl.ds(pl.multiple_of(t * height, height), height)
        pltpu.make_async_copy(
            src.at[chunk, own], dst.at[chunk, own], recv_sem.at[chunk]
        ).start()

    def send_d(part, chunk, height):
        src, dst, send_sem, recv_sem = part["src"], part["dst"], part["send"], part["recv"]

        def step(at, carry):
            peer = lax.rem(g + at, n_dp)
            pltpu.make_async_remote_copy(
                src_ref=src.at[chunk, pl.ds(pl.multiple_of(peer * height, height), height)],
                dst_ref=dst.at[chunk, pl.ds(pl.multiple_of(g * height, height), height)],
                send_sem=send_sem.at[chunk],
                recv_sem=recv_sem.at[chunk],
                device_id=(peer, t),
                device_id_type=MESH,
            ).start()
            return carry

        lax.fori_loop(1, n_dp, step, 0)
        own = pl.ds(pl.multiple_of(g * height, height), height)
        pltpu.make_async_copy(
            src.at[chunk, own], dst.at[chunk, own], recv_sem.at[chunk]
        ).start()

    def arrived(part, chunk):
        dst = part["dst"].at[chunk]
        pltpu.make_async_copy(dst, dst, part["recv"].at[chunk]).wait()

    def sent(part, height):
        chunks, tall, _ = part["src"].shape

        def step(chunk, carry):
            most = part["src"].at[chunk, pl.ds(0, tall - height)]
            pltpu.make_async_copy(most, most, part["send"].at[chunk]).wait()
            return carry

        lax.fori_loop(0, chunks, step, 0)

    def columns_of(chunk, size):
        return pl.ds(pl.multiple_of(chunk * size, size), size)

    down = iota((rows, rows), 0)
    across = iota((rows, rows), 1)
    diagonal = down == across
    before = down < across

    def to_column(row):
        return jnp.sum(jnp.where(diagonal, row, 0), axis=1, keepdims=True)

    def to_row(column):
        return jnp.sum(jnp.where(diagonal, column, 0), axis=0, keepdims=True)

    def count(mask):
        return jnp.sum(jnp.where(mask, 1, 0), axis=0, keepdims=True)

    ids = ids_ref[...]
    ids_col = to_column(ids)
    owner_col = jnp.sum(jnp.where(ids_col == across, slot_ref[...], 0), axis=1, keepdims=True)
    rank = count((ids_col == ids) & before)
    owner = to_row(owner_col)
    column = lax.rem(owner, n_t)
    team = column * RANKS + rank
    team_col = to_column(team)
    live = iota((1, rows), 1) < count_ref[...]
    earlier = count((team_col == team) & before)
    firsts = count((team_col == column * RANKS) & (down < count_ref[...]))
    top = plan.tight - 1 - earlier
    over = live & (rank == 1) & (top < firsts)
    if plan.rest:
        code = jnp.where(over, column * width + firsts - 1 - top, -1)
    else:
        place = jnp.where(rank == 1, top, earlier)
        code = jnp.where(live & ~over, column * width + place, -1)

    def pack(unit, chunk):
        part = unit["go_z"]["src"]
        part[chunk] = dot(unit["pack"][...], x_ref[:, columns_of(chunk, part.shape[2])]).astype(BF16)

    for at, (lo, hi, _, _) in enumerate(plan.units):
        unit = units[at]
        height = hi - lo
        chunks = unit["go_z"]["src"].shape[0]
        spot = iota((n_t * height, 1), 0)
        spot = lax.div(spot, height) * width + lo + lax.rem(spot, height)
        unit["pack"][...] = one_hot(spot == code)
        pack(unit, 0)
        if at == 0:
            pl.semaphore_wait(barrier, n_dp + n_t - 2)

        def start_in(chunk, carry, unit=unit, height=height, chunks=chunks):
            send_z(unit["go_z"], chunk, height)

            @pl.when(chunk < chunks - 1)
            def _():
                pack(unit, chunk + 1)

            return carry

        lax.fori_loop(0, chunks, start_in, 0)

    if flag is not None:
        tile = flag["src"].shape[0]
        most = jnp.max(jnp.where(over, 1.0, 0.0), axis=1, keepdims=True)
        flag["src"][...] = jnp.broadcast_to(most, flag["src"].shape)
        spot = pl.ds(pl.multiple_of(g * tile, tile), tile)

        def tell(step, carry):
            pltpu.make_async_remote_copy(
                src_ref=flag["src"],
                dst_ref=flag["dst"].at[spot],
                send_sem=flag["send"],
                recv_sem=flag["recv"],
                device_id=(lax.rem(g + step, n_dp), t),
                device_id_type=MESH,
            ).start()
            return carry

        lax.fori_loop(1, n_dp, tell, 0)
        pltpu.make_async_copy(flag["src"], flag["dst"].at[spot], flag["recv"]).start()

    code_col = to_column(code)
    rank_col = lax.rem(team_col, RANKS)
    team_row, team_column = lax.div(owner, n_t) * order, lax.div(owner_col, n_t) * order
    first = t * width

    def build_spread(at):
        lo, hi, copies, _ = plan.units[at]
        height = hi - lo
        mat = units[at]["spread"]
        line = team_column * copies + 1 + (rank_col if copies > 1 else 0)
        lane = iota((1, n_t * height), 1)
        here = code_col == first + lo + lax.rem(lane, height)
        key = jnp.sum(jnp.where(here, line, 0), axis=0, keepdims=True)
        key = jnp.where(key > 0, key - 1 + lax.div(lane, height) * copies, -1)
        mat[...] = one_hot(iota(mat.shape, 0) == key)

    def build_gather(at):
        lo, hi, copies, _ = plan.units[at]
        height = hi - lo
        mat = units[at]["gather"]
        line = team_row * copies + 1 + (rank if copies > 1 else 0)
        spot = iota((n_t * height, 1), 0)
        here = code == first + lo + lax.rem(spot, height)
        key = jnp.sum(jnp.where(here, line, 0), axis=1, keepdims=True)
        key = jnp.where(key > 0, key - 1 + lax.div(spot, height) * copies, -1)
        mat[...] = one_hot(iota(mat.shape, 1) == key)

    def build_place(at):
        lo, hi, _, _ = plan.units[at]
        height = hi - lo
        lane = iota((1, n_t * height), 1)
        lane = lax.div(lane, height) * width + lo + lax.rem(lane, height)
        units[at]["place"][...] = one_hot(code_col == lane)

    def build_mix(at):
        copies = plan.units[at][2]
        mat = units[at]["mix"]
        side = mat.shape[0]
        unit_of = lax.rem(lax.div(iota((side, order), 0), copies), order)
        pick = one_hot(unit_of == iota((side, order), 1))
        contract = (((1,), (1,)), ((), ()))
        tall = lax.dot_general(pick, a_ref[...], contract, preferred_element_type=jnp.float32)
        wide = lax.dot_general(
            tall.astype(BF16), pick, contract, preferred_element_type=jnp.float32
        )
        one, two = iota((side, side), 0), iota((side, side), 1)
        same = (lax.div(one, order * copies) == lax.div(two, order * copies)) & (
            lax.rem(one, copies) == lax.rem(two, copies)
        )
        mat[...] = jnp.where(same, wide, 0.0).astype(BF16)

    def spread(at):
        unit = units[at]
        copies = plan.units[at][2]

        def step(chunk, carry):
            arrived(unit["go_z"], chunk)
            unit["go_d"]["src"][chunk] = dot(
                unit["spread"][...], unit["go_z"]["dst"][chunk]
            ).astype(BF16)
            send_d(unit["go_d"], chunk, order * copies)
            return carry

        lax.fori_loop(0, unit["go_z"]["src"].shape[0], step, 0)

    def mix(at):
        unit = units[at]
        side = unit["mix"].shape[0]
        chunks, lines, cols = unit["go_d"]["dst"].shape

        def step(chunk, carry):
            arrived(unit["go_d"], chunk)
            for low in range(0, lines, side):
                unit["mixed"][low : low + side, columns_of(chunk, cols)] = dot(
                    unit["mix"][...], unit["go_d"]["dst"][chunk, low : low + side, :]
                ).astype(BF16)
            return carry

        lax.fori_loop(0, chunks, step, 0)

    def start_out(at, chunk):
        unit = units[at]
        unit["back_d"]["src"][chunk] = dot(
            unit["mixed"][...], b_ref[:, columns_of(chunk, out_cols)]
        ).astype(BF16)
        send_d(unit["back_d"], chunk, order * plan.units[at][2])

    def relay(at, start, stop):
        unit = units[at]
        lo, hi, _, _ = plan.units[at]

        def step(chunk, carry):
            arrived(unit["back_d"], chunk)
            unit["back_z"]["src"][chunk] = dot(
                unit["gather"][...], unit["back_d"]["dst"][chunk]
            ).astype(BF16)
            send_z(unit["back_z"], chunk, hi - lo)

            @pl.when(chunk + 2 < out_chunks)
            def _():
                start_out(at, chunk + 2)

            return carry

        lax.fori_loop(start, stop, step, 0)

    build_spread(0)
    build_mix(0)
    build_gather(0)
    spread(0)
    mix(0)
    start_out(0, 0)
    start_out(0, 1)
    if plan.rest:
        build_place(0)
        relay(0, 0, out_chunks)
    else:
        build_spread(1)
        relay(0, 0, 2)
        build_mix(1)
        spread(1)
        relay(0, 2, 4)
        build_gather(1)
        mix(1)
        start_out(1, 0)
        relay(0, 4, out_chunks - 1)
        start_out(1, 1)
        relay(0, out_chunks - 1, out_chunks)
        relay(1, 0, out_chunks)
        build_place(0)
        build_place(1)

    def place_chunk(chunk, carry):
        for unit in units:
            arrived(unit["back_z"], chunk)
        out_ref[:, columns_of(chunk, out_cols)] = total(
            dot(unit["place"][...], unit["back_z"]["dst"][chunk]) for unit in units
        ).astype(BF16)
        return carry

    lax.fori_loop(0, out_chunks, place_chunk, 0)

    if flag is not None:
        pltpu.make_async_copy(flag["dst"], flag["dst"], flag["recv"]).wait()
        over_ref[...] = jnp.max(flag["dst"][...], axis=0, keepdims=True).astype(I32)
        part = flag["dst"].at[pl.ds(0, (n_dp - 1) * flag["src"].shape[0])]
        pltpu.make_async_copy(part, part, flag["send"]).wait()
    for unit, (lo, hi, copies, _) in zip(units, plan.units):
        sent(unit["go_z"], hi - lo)
        sent(unit["go_d"], order * copies)
        sent(unit["back_d"], order * copies)
        sent(unit["back_z"], hi - lo)


def exchange(rest, ids, slot, counts, rows_in, small, large):
    n_dp = lax.axis_size("dp")
    n_t = lax.axis_size("tensor")
    plan = Plan(n_dp, rest)
    rows, in_width = rows_in.shape
    order = small.shape[0]
    out_width = large.shape[1]
    out_chunks = max(4, out_width // OUT_CHUNK)

    def buffer(*shape):
        return pltpu.VMEM(shape, BF16)

    def copied(chunks, tall, cols):
        return {
            "src": buffer(chunks, tall, cols),
            "dst": buffer(chunks, tall, cols),
            "send": pltpu.SemaphoreType.DMA((chunks,)),
            "recv": pltpu.SemaphoreType.DMA((chunks,)),
        }

    def unit_scratch(lo, hi, copies, cols):
        tall = n_t * (hi - lo)
        lines = n_dp * order * copies
        side = min(SIDE, lines)
        in_chunks = max(1, in_width // cols)
        return {
            "pack": buffer(tall, rows),
            "spread": buffer(lines, tall),
            "gather": buffer(tall, lines),
            "place": buffer(rows, tall),
            "mix": buffer(side, side),
            "mixed": buffer(lines, in_width),
            "go_z": copied(in_chunks, tall, in_width // in_chunks),
            "go_d": copied(in_chunks, lines, in_width // in_chunks),
            "back_d": copied(out_chunks, lines, out_width // out_chunks),
            "back_z": copied(out_chunks, tall, out_width // out_chunks),
        }

    scratch = [[unit_scratch(*unit) for unit in plan.units]]
    out_shape = [jax.ShapeDtypeStruct((rows, out_width), BF16)]
    if not rest:
        out_shape.append(jax.ShapeDtypeStruct((1, 128), I32))
        scratch.append(
            {
                "src": pltpu.VMEM((8, 128), jnp.float32),
                "dst": pltpu.VMEM((8 * n_dp, 128), jnp.float32),
                "send": pltpu.SemaphoreType.DMA,
                "recv": pltpu.SemaphoreType.DMA,
            }
        )
    return pl.pallas_call(
        functools.partial(exchange_kernel, n_dp, n_t, plan),
        out_shape=out_shape,
        in_specs=[pl.BlockSpec(memory_space=pltpu.VMEM)] * 6,
        out_specs=[pl.BlockSpec(memory_space=pltpu.VMEM)] * len(out_shape),
        scratch_shapes=scratch,
        compiler_params=pltpu.CompilerParams(
            collective_id=1 if rest else 0,
            has_side_effects=True,
            vmem_limit_bytes=56 * 1024 * 1024,
        ),
        cost_estimate=pl.CostEstimate(
            flops=2 * RANKS * n_dp * order * in_width * out_width,
            bytes_accessed=10_000_000,
            transcendentals=0,
        ),
    )(ids, slot, counts, rows_in, small, large)


def on_device(rows_in, adapter_ids, row_counts, adapter_slot, adapter_a, adapter_b):
    args = (
        adapter_ids[None, :],
        adapter_slot[None, :],
        row_counts[None, :],
        rows_in,
        adapter_a[0],
        adapter_b[0],
    )
    done, over = exchange(False, *args)
    return lax.cond(
        over[0, 0] > 0,
        lambda done, *args: done + exchange(True, *args)[0],
        lambda done, *args: done,
        done,
        *args,
    )


def solution(mesh):
    return jax.shard_map(
        on_device,
        mesh=mesh,
        in_specs=(
            P("dp", "tensor"),
            P("dp"),
            P("dp"),
            P(),
            P(("dp", "tensor"), None, None),
            P(("dp", "tensor"), None, None),
        ),
        out_specs=P("dp", "tensor"),
        check_vma=False,
    )
```

time: 185 us -> 179 us (0.968)
  Pallas kernels: 182 us -> 177 us
    pallas_call x1, Pallas kernels: 182 us -> 177 us  [exchange(): pl.pallas_call(functools.partial(exchange_kernel, n_dp, n_t, plan), out_s...]
where the time goes in v4:
time: 179 us
  Pallas kernels  177 us (99%)
    pallas_call x1, Pallas kernels, exchange(): pl.pallas_call(functools.partial(exchange_kernel, n_dp, n_t, plan), out_s...  177 us

profile of v4, /device:TPU:1, one launch (start us, length us, event | category | flops | bytes accessed | tf_op | source)
XLA Modules:
  0.0 179.3 jit_solution(12480910296266989398)
XLA Ops:
  0.7 0.0 copy-start
  0.7 0.0 copy-start.1
  0.7 0.0 copy-start.2
  0.7 0.0 copy-start.3
  0.7 0.0 copy-start.4
  0.7 176.7 %shard_map.66 = (bf16[512,1792]{1,0:T(8,128)(2,1)S(1)}, s32[1,128]{1,0:T(1,128)}) custom-call(s32[1,512]{1,0:T(1,128)} %bitcast.12, s32[1,512]{1,0:T(1,128)} %bitcast.14, s32[1,1]{1,0:T(1,128)} %bitcast.7.count_ref, bf16[512,512]{1,0:T(8,128)(2,1)} %x_ref.1, bf16[16,16]{1,0:T(8,128)(2,1)} %bitcast.10, bf16[512,1792]{1,0:T(8,128)(2,1)} %bitcast.8), custom_call_target="tpu_custom_call" | custom-call | flops 1879048192 | bytes 10000000 | tf_op jit(solution)/shard_map/pallas_call | solution.py:423
  178.0 0.0 copy-done
  178.0 0.0 copy-done.1
  178.0 0.0 copy-done.2
  178.0 0.0 copy-done.3
  178.1 0.0 copy-done.4
  178.1 1.2 copy.13
  (1 shorter events, 0.0 us)
Async XLA Ops:
  0.7 177.4 %copy-start = (bf16[1,512,1792]{2,1,0:T(8,128)(2,1)S(1)}, bf16[1,512,1792]{2,1,0:T(8,128)(2,1)}, u32[]{:S(2)}) copy-start(bf16[1,512,1792]{2,1,0:T(8,128)(2,1)} %param.13) | copy-start | bytes 5505028
  0.7 177.4 %copy-start.1 = (bf16[512,512]{1,0:T(8,128)(2,1)S(1)}, bf16[512,512]{1,0:T(8,128)(2,1)}, u32[]{:S(2)}) copy-start(bf16[512,512]{1,0:T(8,128)(2,1)} %x_ref.1) | copy-start | bytes 1572868
  0.7 177.4 %copy-start.2 = (bf16[1,16,16]{2,1,0:T(8,128)(2,1)S(1)}, bf16[1,16,16]{2,1,0:T(8,128)(2,1)}, u32[]{:S(2)}) copy-start(bf16[1,16,16]{2,1,0:T(8,128)(2,1)} %param.12) | copy-start | bytes 1540
  0.7 177.4 %copy-start.3 = (s32[512]{0:T(512)S(1)}, s32[512]{0:T(512)}, u32[]{:S(2)}) copy-start(s32[512]{0:T(512)} %param.9) | copy-start | bytes 6148
  0.7 177.4 %copy-start.4 = (s32[512]{0:T(512)S(1)}, s32[512]{0:T(512)}, u32[]{:S(2)}) copy-start(s32[512]{0:T(512)} %param.11) | copy-start | bytes 6148
